TPU v7x, 32 devices: a whole 2x2x4 slice. The times are simulated.
32 devices in a mesh: lat: 4 (over y, x), lon: 8 (over z, core).
Axes of the slice: x: 2, y: 2, z: 4, core: 2. Of those that a mesh axis runs over, the one named last changes fastest.
Arguments:
- field: bfloat16 [48, 384, 360], P('lat', None, 'lon'), may hold values from -6 to 6
- support: int32 [48, 3], P('lat'), may hold values from 0 to 47, as said below
- spec_one: float32 [2, 3, 48, 3, 180], P(None, None, 'lat'), may hold values from -3 to 3
- theta_one: float32 [384, 3], replicated, may hold values from -3 to 3
- spec_two: float32 [2, 3, 48, 3, 180], P(None, None, 'lat'), may hold values from -3 to 3
- theta_two: float32 [384, 3], replicated, may hold values from -3 to 3
- norm_gain: float32 [384], replicated, may hold values from 0.25 to 1.75
- w_in: bfloat16 [1536, 384], P('lon'), may hold values from -0.3125 to 0.3125
- w_out: bfloat16 [1536, 384], P('lon'), may hold values from -0.15625 to 0.15625
Outputs:
- result: bfloat16 [48, 384, 360], P('lat', None, 'lon')
Inputs may be any that keep to these rules, and one draw needn't show every extreme that they name: support[i, 0] = i; every other entry lies within 2 rows of i, clipped to the grid.
All inputs are finite; a program needn't handle non-finite values.
Results may differ from a plain program's by a relative error of at most 0.0072.
Values may be sent and summed in bfloat16 or wider, within the bound.
A program may use at most 64 MiB of HBM per device.

v0:
```python
import functools
import math

import jax
import jax.numpy as jnp
import numpy as np
from jax import lax
from jax.experimental import pallas as pl
from jax.experimental.pallas import tpu as pltpu
from jax.sharding import PartitionSpec as P

HALO = 2
MESH = pl.DeviceIdType.MESH
F32 = jnp.float32
BF16 = jnp.bfloat16


def round_up(value, step):
    return -(-value // step) * step


def tables(circle, n, lons, lon_pad, mode_pad):
    half = circle // 2
    grid = np.arange(circle)[:, None] * np.arange(half)[None, :] % circle
    phase = grid.astype(np.float64) * (2.0 * math.pi / circle)
    cos, sin = np.cos(phase), np.sin(phase)
    weights = np.where(np.arange(half) == 0, 1.0, 2.0) / circle
    forward = np.zeros((n, lon_pad, 2, mode_pad), np.float32)
    forward[:, :lons, 0, :half] = cos.reshape(n, lons, half)
    forward[:, :lons, 1, :half] = -sin.reshape(n, lons, half)
    inverse_t = np.zeros((n, lon_pad, 2, mode_pad), np.float32)
    inverse_t[:, :lons, 0, :half] = (cos * weights).reshape(n, lons, half)
    inverse_t[:, :lons, 1, :half] = (-sin * weights).reshape(n, lons, half)
    forward = forward.reshape(n * lon_pad, 2 * mode_pad)
    inverse_t = inverse_t.reshape(n * lon_pad, 2 * mode_pad)
    eye = np.eye(lon_pad, lons, dtype=np.float32)
    return [jnp.asarray(t, BF16) for t in (eye, forward, inverse_t.T, inverse_t)]


def conv_kernel(
    n, n_lat, chans, half,
    support, field, eye, forward, inverse, inverse_t, spec_one, theta_one, spec_two, theta_two, gain,
    out,
    send_t, circ_t, ext_one, ext_two, spectra, packed, first, part, sums, totals, second_t,
    a_send, a_recv, b_send, b_recv, c_send, c_recv, d_send, d_recv, h_send, h_recv,
):
    rows = field.shape[0]
    cp = field.shape[1] // n
    lon_pad = eye.shape[0]
    mode_pad = forward.shape[1] // 2
    me = lax.axis_index("lon")
    lat = lax.axis_index("lat")
    up = lax.rem(lat + 1, n_lat)
    down = lax.rem(lat + n_lat - 1, n_lat)
    per = part.shape[1]

    def peer(o):
        return lax.rem(me + o, n)

    barrier = pltpu.get_barrier_semaphore()
    for o in range(1, n):
        pl.semaphore_signal(barrier, inc=1, device_id=(lat, peer(o)), device_id_type=MESH)
    for side in (up, down):
        pl.semaphore_signal(barrier, inc=1, device_id=(side, me), device_id_type=MESH)

    def block_of(d):
        x = field[:, pl.ds(pl.multiple_of(d * cp, 16), cp), :].reshape(rows * cp, field.shape[2])
        turned = lax.dot_general(eye[...], x, (((1,), (1,)), ((), ())), preferred_element_type=F32)
        return turned.astype(BF16)

    def exchange(srcs, dst, send, recv):
        copies = []
        for o in range(1, n):
            copies.append(pltpu.make_async_remote_copy(
                src_ref=srcs(o), dst_ref=dst, send_sem=send.at[o], recv_sem=recv.at[o],
                device_id=(lat, peer(o)), device_id_type=MESH))
        return copies

    mine = pl.multiple_of(me * lon_pad, 16)
    copies_a = exchange(lambda o: send_t.at[o], circ_t.at[pl.ds(mine, lon_pad)], a_send, a_recv)
    for o in range(1, n):
        send_t[o] = block_of(peer(o))
        if o == 1:
            pl.semaphore_wait(barrier, n + 1)
        copies_a[o - 1].start()
    circ_t[pl.ds(mine, lon_pad)] = block_of(me)
    packed[...] = jnp.zeros_like(packed)
    part[...] = jnp.zeros_like(part)

    own = slice(HALO * cp, (HALO + rows) * cp)

    def halo(ext, which):
        width = HALO * cp
        low = pltpu.make_async_remote_copy(
            src_ref=ext.at[pl.ds(width, width)], dst_ref=ext.at[pl.ds(width + rows * cp, width)],
            send_sem=h_send.at[which, 0], recv_sem=h_recv.at[which, 0],
            device_id=(down, me), device_id_type=MESH)
        high = pltpu.make_async_remote_copy(
            src_ref=ext.at[pl.ds(rows * cp, width)], dst_ref=ext.at[pl.ds(0, width)],
            send_sem=h_send.at[which, 1], recv_sem=h_recv.at[which, 1],
            device_id=(up, me), device_id_type=MESH)
        return low, high

    def mix(ext, halos, spec, theta):
        def dft(start, count):
            x = ext[start * cp:(start + count) * cp, :]
            spectra[start:start + count] = jnp.dot(
                x, forward[...], preferred_element_type=F32).reshape(count, cp, 2 * mode_pad)

        dft(HALO, rows)
        for copy in halos:
            copy.wait_recv()
        dft(0, HALO)
        dft(HALO + rows, HALO)
        th = theta[pl.ds(pl.multiple_of(me * cp, 8), cp), :]
        cols = [th[:, b:b + 1] for b in range(th.shape[1])]

        def row(i, carry):
            p_re = jnp.zeros((cp, half), F32)
            p_im = jnp.zeros((cp, half), F32)
            for k in range(support.shape[1]):
                r = jnp.clip(support[i, k] - lat * rows + HALO, 0, rows + 2 * HALO - 1)
                g = spectra[r]
                g_re, g_im = g[:, :half], g[:, mode_pad:mode_pad + half]
                w_re = sum(cols[b] * spec[0, b, i][k:k + 1, :] for b in range(len(cols)))
                w_im = sum(cols[b] * spec[1, b, i][k:k + 1, :] for b in range(len(cols)))
                p_re += w_re * g_re - w_im * g_im
                p_im += w_re * g_im + w_im * g_re
            packed[i, :, :half] = p_re.astype(BF16)
            packed[i, :, mode_pad:mode_pad + half] = p_im.astype(BF16)
            return carry

        lax.fori_loop(0, rows, row, 0)
        return packed[...].reshape(rows * cp, 2 * mode_pad)

    for copy in copies_a:
        copy.wait_recv()
    ext_one[own, :] = circ_t[...].T
    halo_one = halo(ext_one, 0)
    for copy in halo_one:
        copy.start()
    spectrum = mix(ext_one, halo_one, spec_one, theta_one)
    values = jnp.dot(spectrum, inverse[...], preferred_element_type=F32).astype(BF16)
    first[...] = values.reshape(first.shape)

    for i in range(rows):
        v = first[i].astype(F32)
        part[i // per, i % per] = jnp.sum(v, axis=0)
        j = rows + i
        part[j // per, j % per] = jnp.sum(v * v, axis=0)
    copies_b = exchange(lambda o: part.at[peer(o)], sums.at[me], b_send, b_recv)
    for copy in copies_b:
        copy.start()
    sums[me] = part[me]
    for copy in copies_b:
        copy.wait_recv()
    totals[me] = jnp.sum(sums[...], axis=0)
    copies_c = exchange(lambda o: totals.at[me], totals.at[me], c_send, c_recv)
    for copy in copies_c:
        copy.start()
    for copy in copies_c:
        copy.wait_recv()
    scale = gain[pl.ds(pl.multiple_of(me * cp, 8), cp), :]
    halo_two = halo(ext_two, 1)

    def normalise(i):
        j = rows + i
        mean = totals[i // per, i % per][None, :] * (1.0 / chans)
        meansq = totals[j // per, j % per][None, :] * (1.0 / chans)
        v = first[i].astype(F32)
        v = (v - mean) * lax.rsqrt(meansq - mean * mean + 1e-05) * scale
        ext_two[(HALO + i) * cp:(HALO + i + 1) * cp, :] = v.astype(BF16)

    edges = list(range(HALO)) + list(range(rows - HALO, rows))
    for i in edges:
        normalise(i)
    for copy in halo_two:
        copy.start()
    for i in range(HALO, rows - HALO):
        normalise(i)
    spectrum = mix(ext_two, halo_two, spec_two, theta_two)
    second_t[...] = lax.dot_general(
        inverse_t[...], spectrum, (((1,), (1,)), ((), ())), preferred_element_type=F32
    ).astype(BF16).reshape(second_t.shape)
    copies_d = exchange(lambda o: second_t.at[peer(o)], out.at[me], d_send, d_recv)
    for copy in copies_d:
        copy.start()
    out[me] = second_t[me]
    for copy in copies_d:
        copy.wait_recv()
    for copy in copies_a + copies_b + copies_c + copies_d:
        copy.wait_send()
    for copy in halo_one + halo_two:
        copy.wait_send()


def shards(n, n_lat, field, support, spec_one, theta_one, spec_two, theta_two, norm_gain, w_in, w_out):
    rows, chans, lons = field.shape
    circle = lons * n
    half = circle // 2
    part = chans // n
    cp = round_up(part, 16)
    lon_pad = round_up(lons, 16)
    mode_pad = round_up(half, 128)
    eye, forward, inverse, inverse_t = tables(circle, n, lons, lon_pad, mode_pad)

    def spread(x, axis):
        if cp == part:
            return x
        shape = x.shape
        x = x.reshape(shape[:axis] + (n, part) + shape[axis + 1:])
        pads = [(0, 0)] * x.ndim
        pads[axis + 1] = (0, cp - part)
        return jnp.pad(x, pads).reshape(shape[:axis] + (n * cp,) + shape[axis + 1:])

    per = -(-2 * rows // n)
    lanes = n * lon_pad
    vmem = pl.BlockSpec(memory_space=pltpu.VMEM)
    smem = pl.BlockSpec(memory_space=pltpu.SMEM)
    pair = pltpu.SemaphoreType.DMA((n,))
    out = pl.pallas_call(
        functools.partial(conv_kernel, n, n_lat, chans, half),
        out_shape=jax.ShapeDtypeStruct((n, lon_pad, rows * cp), BF16),
        in_specs=[smem] + [vmem] * 10,
        out_specs=vmem,
        scratch_shapes=[
            pltpu.VMEM((n, lon_pad, rows * cp), BF16),
            pltpu.VMEM((lanes, rows * cp), BF16),
            pltpu.VMEM(((rows + 2 * HALO) * cp, lanes), BF16),
            pltpu.VMEM(((rows + 2 * HALO) * cp, lanes), BF16),
            pltpu.VMEM((rows + 2 * HALO, cp, 2 * mode_pad), F32),
            pltpu.VMEM((rows, cp, 2 * mode_pad), BF16),
            pltpu.VMEM((rows, cp, lanes), BF16),
            pltpu.VMEM((n, per, lanes), F32),
            pltpu.VMEM((n, per, lanes), F32),
            pltpu.VMEM((n, per, lanes), F32),
            pltpu.VMEM((n, lon_pad, rows * cp), BF16),
        ] + [pair] * 8 + [pltpu.SemaphoreType.DMA((2, 2))] * 2,
        compiler_params=pltpu.CompilerParams(
            collective_id=0, has_side_effects=True, vmem_limit_bytes=50 * 2**20),
        name="convs",
    )(
        support, spread(field, 1), eye, forward, inverse, inverse_t,
        spec_one, spread(theta_one, 0), spec_two, spread(theta_two, 0), spread(norm_gain, 0)[:, None],
    )
    piece_in = lax.all_gather(w_in, "lon", axis=0, tiled=True)
    piece_out = lax.all_gather(w_out, "lon", axis=0, tiled=True)
    cells = out.reshape(n, lon_pad, rows, cp)[:, :lons, :, :part]
    cells = cells.transpose(2, 0, 3, 1).reshape(rows, chans, lons)
    hidden = jax.nn.gelu(
        jnp.einsum("hcl,fc->hfl", cells, piece_in, preferred_element_type=F32)
    ).astype(BF16)
    update = jnp.einsum("hfl,fc->hcl", hidden, piece_out, preferred_element_type=F32)
    return (field.astype(F32) + update).astype(BF16)


def solution(mesh):
    in_specs = (
        P("lat", None, "lon"),
        P("lat", None),
        P(None, None, "lat", None, None),
        P(),
        P(None, None, "lat", None, None),
        P(),
        P(),
        P("lon", None),
        P("lon", None),
    )
    body = functools.partial(shards, mesh.shape["lon"], mesh.shape["lat"])
    return jax.shard_map(
        body, mesh=mesh, in_specs=in_specs, out_specs=P("lat", None, "lon"), check_vma=False)
```

profile of v0, /device:TPU:1, one launch (start us, length us, event | category | flops | bytes accessed | tf_op | source)
XLA Modules:
  0.0 87.7 jit_solution(8889282035295632585)
XLA Ops:
  6.5 0.0 copy-start.5
  6.5 0.0 copy-start.6
  6.5 0.0 copy-start.9
  6.5 0.0 copy-start.7
  6.5 0.0 all-gather.3.cloned.1.call-start
  6.6 0.7 all-gather.3.cloned.1.call-update
  7.3 0.0 copy-start.8
  7.3 0.0 all-gather.5.cloned.1.call-start
  7.3 0.7 all-gather.5.cloned.1.call-update
  8.0 0.0 copy-start.10
  8.0 0.0 copy-start
  8.1 0.0 copy-start.3
  8.1 1.8 %copy.22.field = bf16[12,384,45]{2,1,0:T(8,128)(2,1)S(1)} copy(bf16[12,384,45]{1,2,0:T(8,128)(2,1)} %param.13) | data formatting | bytes 829440 | tf_op args[0]
  9.8 0.0 copy-done.5
  9.8 0.1 copy.23.spec_one
  9.9 0.0 copy-done.6
  9.9 0.1 copy.25.spec_two
  10.0 0.0 copy-done.9
  10.0 0.1 broadcast_in_dim.4.gain
  10.1 0.0 copy-done.7
  10.2 0.1 copy.24.theta_one
  10.3 0.0 copy-done.8
  10.3 0.1 copy.26.theta_two
  10.5 0.0 copy-done.10
  10.5 0.1 copy.21.support
  10.6 0.0 copy-done
  10.6 0.0 copy-done.3
  10.6 0.0 copy-start.1
  10.6 1.0 %copy-done.1 = bf16[512,384]{1,0:T(8,128)(2,1)S(1)} copy-done((bf16[512,384]{1,0:T(8,128)(2,1)S(1)}, bf16[512,384]{1,0:T(8,128)(2,1)}, u32[]{:S(2)}) %copy-start.1) | copy-done | bytes 393240
  11.6 0.0 copy-start.2
  11.6 1.0 %copy-done.2 = bf16[384,512]{1,0:T(8,128)(2,1)S(1)} copy-done((bf16[384,512]{1,0:T(8,128)(2,1)S(1)}, bf16[384,512]{1,0:T(8,128)(2,1)}, u32[]{:S(2)}) %copy-start.2) | copy-done | bytes 393240
  12.6 60.6 %convs.1 = bf16[8,48,576]{2,1,0:T(8,128)(2,1)S(1)} custom-call(s32[12,3]{1,0:T(8,128)S(1)} %copy.21.support, bf16[12,384,45]{2,1,0:T(8,128)(2,1)S(1)} %copy.22.field, bf16[48,45]{1,0:T(8,128)(2,1)S(1)} %copy-done.3, bf16[384,512]{1,0:T(8,128)(2,1)S(1)} %copy-done, bf16[512,384]{1,0:T(8,128)(2,1)S(1)} %copy-done.1, bf16[384,512]{1,0:T(8,128)(2,1)S(1)} %copy-done.2, ...), custom_call_target="tpu_custom_call" | custom-call | tf_op jit(solution)/shard_map/convs/pallas_call | solution.py:221
  73.2 1.5 %reshape.6 = bf16[8,48,12,48]{3,2,1,0:T(8,128)(2,1)S(1)} reshape(bf16[8,48,576]{2,1,0:T(8,128)(2,1)S(1)} %convs.1) | data formatting | bytes 884736 | tf_op jit(solution)/shard_map/reshape | solution.py:248
  74.7 0.3 slice_bitcast_fusion
  75.0 0.0 copy-start.4
  75.0 0.3 copy.28
  75.3 1.0 %reshape.7 = bf16[12,384,45]{1,2,0:T(8,128)(2,1)S(1)} reshape(bf16[12,8,48,45]{2,1,3,0:T(8,128)(2,1)S(1)} %copy.28) | data formatting | bytes 829440 | tf_op jit(solution)/shard_map/reshape | solution.py:249
  76.3 0.0 all-gather.3.cloned.1.call-done
  76.4 0.0 all-gather.5.cloned.1.call-done
  76.4 0.0 copy-done.4
  76.4 4.5 %fusion.9 = bf16[12,384,45]{1,2,0:T(8,128)(2,1)} fusion(bf16[12,384,45]{1,2,0:T(8,128)(2,1)S(1)} %reshape.7, bf16[1536,384]{1,0:T(8,128)(2,1)} %all-gather.5.cloned.1.call-done, bf16[1536,384]{1,0:T(8,128)(2,1)} %all-gather.3.cloned.1.call-done, bf16[12,384,45]{1,2,0:T(8,128)(2,1)S(1)} %copy-done.4), kind=kOutput, calls=%fused_computation.12 | convolution fusion | flops 1282106880 | bytes 3603456 | tf_op jit(solution)/shard_map/hfl,fc->hcl/dot_general | solution.py:253
Async XLA Ops:
  6.5 3.3 %copy-start.5 = (f32[2,3,12,3,180]{4,0,3,2,1:T(2,128)S(1)}, f32[2,3,12,3,180]{4,0,3,2,1:T(2,128)}, u32[]{:S(2)}) copy-start(f32[2,3,12,3,180]{4,0,3,2,1:T(2,128)} %param.15) | copy-start | bytes 466564
  6.5 3.4 %copy-start.6 = (f32[2,3,12,3,180]{4,0,3,2,1:T(2,128)S(1)}, f32[2,3,12,3,180]{4,0,3,2,1:T(2,128)}, u32[]{:S(2)}) copy-start(f32[2,3,12,3,180]{4,0,3,2,1:T(2,128)} %param.17) | copy-start | bytes 466564
  6.5 3.5 %copy-start.9 = (f32[384]{0:T(512)S(1)}, f32[384]{0:T(512)}, u32[]{:S(2)}) copy-start(f32[384]{0:T(512)} %param.19) | copy-start | bytes 4612
  6.5 3.6 %copy-start.7 = (f32[384,3]{0,1:T(4,128)S(1)}, f32[384,3]{0,1:T(4,128)}, u32[]{:S(2)}) copy-start(f32[384,3]{0,1:T(4,128)} %param.16) | copy-start | bytes 13828
  6.5 69.8 %all-gather.3.cloned.1.call-start = ((), (), s32[]{:S(2)}) async-start(), calls=%async_computation | async-start | bytes 1327104 | tf_op jit(solution)/shard_map/all_gather | solution.py:246
  7.3 3.0 %copy-start.8 = (f32[384,3]{0,1:T(4,128)S(1)}, f32[384,3]{0,1:T(4,128)}, u32[]{:S(2)}) copy-start(f32[384,3]{0,1:T(4,128)} %param.18) | copy-start | bytes 13828
  7.3 69.1 %all-gather.5.cloned.1.call-start = ((), (), s32[]{:S(2)}) async-start(), calls=%async_computation.1 | async-start | bytes 1327104 | tf_op jit(solution)/shard_map/all_gather | solution.py:247
  8.0 2.4 %copy-start.10 = (s32[12,3]{0,1:T(4,128)S(1)}, s32[12,3]{0,1:T(4,128)}, u32[]{:S(2)}) copy-start(s32[12,3]{0,1:T(4,128)} %param.14) | copy-start | bytes 436
  8.0 2.5 %copy-start = (bf16[384,512]{1,0:T(8,128)(2,1)S(1)}, bf16[384,512]{1,0:T(8,128)(2,1)}, u32[]{:S(2)}) copy-start(bf16[384,512]{1,0:T(8,128)(2,1)} %constant.17.clone.forward) | copy-start | bytes 1179652
  8.1 2.5 %copy-start.3 = (bf16[48,45]{1,0:T(8,128)(2,1)S(1)}, bf16[48,45]{1,0:T(8,128)(2,1)}, u32[]{:S(2)}) copy-start(bf16[48,45]{1,0:T(8,128)(2,1)} %constant.16.clone.eye) | copy-start | bytes 12964
  10.6 1.0 %copy-start.1 = (bf16[512,384]{1,0:T(8,128)(2,1)S(1)}, bf16[512,384]{1,0:T(8,128)(2,1)}, u32[]{:S(2)}) copy-start(bf16[512,384]{1,0:T(8,128)(2,1)} %constant.18.clone.inverse) | copy-start | bytes 1179652
  11.6 1.0 %copy-start.2 = (bf16[384,512]{1,0:T(8,128)(2,1)S(1)}, bf16[384,512]{1,0:T(8,128)(2,1)}, u32[]{:S(2)}) copy-start(bf16[384,512]{1,0:T(8,128)(2,1)} %constant.19.clone.inverse_t) | copy-start | bytes 1179652
  75.0 1.4 %copy-start.4 = (bf16[12,384,45]{1,2,0:T(8,128)(2,1)S(1)}, bf16[12,384,45]{1,2,0:T(8,128)(2,1)}, u32[]{:S(2)}) copy-start(bf16[12,384,45]{1,2,0:T(8,128)(2,1)} %param.13) | copy-start | bytes 1244164
Sparse Core Ops, SparseCore 0:
  9.0 32.2 all-gather.2
  42.9 29.6 all-gather.4
where the time goes:
time: 88.6 us; the launch traced here: 87.7 us
  Pallas kernels  60.6 us (68%)
  between operations  13.6 us (15%)
  local copies, waits for them, and re-layouts  7.52 us (8%)
  matrix products  4.49 us (5%)
  waiting for transfers between devices  1.42 us (2%)
    pallas_call x1, Pallas kernels, shards(): pl.pallas_call(functools.partial(conv_kernel, n, n_lat, chans, half), out...  60.6 us
    dot_general x1, matrix products, shards(): jnp.einsum('hfl,fc->hcl', hidden, piece_out, preferred_element_type=F32)  4.49 us
    unnamed x28, local copies, waits for them, and re-layouts  4.31 us
  transfers between devices with their start and end apart: 2, of which 0 were waited for; matrix products, arithmetic and copies ran while one was open for 6% of the time, Pallas kernels for 69%

commit v1 on v0

--- a/solution.py
+++ b/solution.py
@@ -10,6 +10,7 @@
 from jax.sharding import PartitionSpec as P
 
 HALO = 2
+CORES = 2
 MESH = pl.DeviceIdType.MESH
 F32 = jnp.float32
 BF16 = jnp.bfloat16
@@ -38,11 +39,12 @@
 
 
 def conv_kernel(
-    n, n_lat, chans, half,
-    support, field, eye, forward, inverse, inverse_t, spec_one, theta_one, spec_two, theta_two, gain,
-    out,
+    n, n_lat, chans, half, gather,
+    support, field, eye, forward, inverse, inverse_t, spec_one, theta_one, spec_two, theta_two, gain, w_in, w_out,
+    out, all_in, all_out,
     send_t, circ_t, ext_one, ext_two, spectra, packed, first, part, sums, totals, second_t,
     a_send, a_recv, b_send, b_recv, c_send, c_recv, d_send, d_recv, h_send, h_recv,
+    u_send, u_recv, v_send, v_recv, w_send, w_recv,
 ):
     rows = field.shape[0]
     cp = field.shape[1] // n
@@ -60,8 +62,9 @@
     barrier = pltpu.get_barrier_semaphore()
     for o in range(1, n):
         pl.semaphore_signal(barrier, inc=1, device_id=(lat, peer(o)), device_id_type=MESH)
-    for side in (up, down):
-        pl.semaphore_signal(barrier, inc=1, device_id=(side, me), device_id_type=MESH)
+    for o in range(1, n_lat):
+        pl.semaphore_signal(
+            barrier, inc=1, device_id=(lax.rem(lat + o, n_lat), me), device_id_type=MESH)
 
     def block_of(d):
         x = field[:, pl.ds(pl.multiple_of(d * cp, 16), cp), :].reshape(rows * cp, field.shape[2])
@@ -81,11 +84,37 @@
     for o in range(1, n):
         send_t[o] = block_of(peer(o))
         if o == 1:
-            pl.semaphore_wait(barrier, n + 1)
+            pl.semaphore_wait(barrier, n + n_lat - 2)
         copies_a[o - 1].start()
     circ_t[pl.ds(mine, lon_pad)] = block_of(me)
     packed[...] = jnp.zeros_like(packed)
     part[...] = jnp.zeros_like(part)
+
+    pairs = ((w_in, all_in), (w_out, all_out)) if gather else ()
+    core = lax.rem(me, CORES)
+    chip = me // CORES
+
+    def remote(src, dst, send, recv, device):
+        return pltpu.make_async_remote_copy(
+            src_ref=src, dst_ref=dst, send_sem=send, recv_sem=recv,
+            device_id=device, device_id_type=MESH)
+
+    copies_u, copies_v, copies_w = [], [], []
+    for m, (shard, whole) in enumerate(pairs):
+        piece = whole.shape[3]
+        share = pl.ds(pl.multiple_of(lat * piece, 16), piece)
+        for o in range(1, n // CORES):
+            copies_u.append(remote(
+                shard.at[share], whole.at[core, lat, chip], u_send.at[m, o], u_recv.at[m, o],
+                (lat, peer(CORES * o))))
+        for o in range(1, n_lat):
+            copies_v.append(remote(
+                whole.at[core, lat], whole.at[core, lat], v_send.at[m, o], v_recv.at[m, o],
+                (lax.rem(lat + o, n_lat), me)))
+        copies_w.append(remote(
+            whole.at[core], whole.at[core], w_send.at[m], w_recv.at[m],
+            (lat, me + 1 - 2 * core)))
+        whole[core, lat, chip] = shard[share, :]
 
     own = slice(HALO * cp, (HALO + rows) * cp)
 
@@ -139,6 +168,8 @@
     halo_one = halo(ext_one, 0)
     for copy in halo_one:
         copy.start()
+    for copy in copies_u:
+        copy.start()
     spectrum = mix(ext_one, halo_one, spec_one, theta_one)
     values = jnp.dot(spectrum, inverse[...], preferred_element_type=F32).astype(BF16)
     first[...] = values.reshape(first.shape)
@@ -152,6 +183,10 @@
     for copy in copies_b:
         copy.start()
     sums[me] = part[me]
+    for copy in copies_u:
+        copy.wait_recv()
+    for copy in copies_v:
+        copy.start()
     for copy in copies_b:
         copy.wait_recv()
     totals[me] = jnp.sum(sums[...], axis=0)
@@ -185,10 +220,14 @@
     copies_d = exchange(lambda o: second_t.at[peer(o)], out.at[me], d_send, d_recv)
     for copy in copies_d:
         copy.start()
+    for copy in copies_v:
+        copy.wait_recv()
+    for copy in copies_w:
+        copy.start()
     out[me] = second_t[me]
-    for copy in copies_d:
-        copy.wait_recv()
-    for copy in copies_a + copies_b + copies_c + copies_d:
+    for copy in copies_d + copies_w:
+        copy.wait_recv()
+    for copy in copies_a + copies_b + copies_c + copies_d + copies_u + copies_v + copies_w:
         copy.wait_send()
     for copy in halo_one + halo_two:
         copy.wait_send()
@@ -218,11 +257,16 @@
     vmem = pl.BlockSpec(memory_space=pltpu.VMEM)
     smem = pl.BlockSpec(memory_space=pltpu.SMEM)
     pair = pltpu.SemaphoreType.DMA((n,))
-    out = pl.pallas_call(
-        functools.partial(conv_kernel, n, n_lat, chans, half),
-        out_shape=jax.ShapeDtypeStruct((n, lon_pad, rows * cp), BF16),
-        in_specs=[smem] + [vmem] * 10,
-        out_specs=vmem,
+    piece = w_in.shape[0] // n_lat
+    gather = n % CORES == 0 and w_in.shape[0] % n_lat == 0 and piece % 16 == 0
+    if not gather:
+        piece = 16
+    weights = jax.ShapeDtypeStruct((CORES, n_lat, n // CORES, piece, chans), BF16)
+    out, piece_in, piece_out = pl.pallas_call(
+        functools.partial(conv_kernel, n, n_lat, chans, half, gather),
+        out_shape=(jax.ShapeDtypeStruct((n, lon_pad, rows * cp), BF16), weights, weights),
+        in_specs=[smem] + [vmem] * 12,
+        out_specs=(vmem, vmem, vmem),
         scratch_shapes=[
             pltpu.VMEM((n, lon_pad, rows * cp), BF16),
             pltpu.VMEM((lanes, rows * cp), BF16),
@@ -235,16 +279,22 @@
             pltpu.VMEM((n, per, lanes), F32),
             pltpu.VMEM((n, per, lanes), F32),
             pltpu.VMEM((n, lon_pad, rows * cp), BF16),
-        ] + [pair] * 8 + [pltpu.SemaphoreType.DMA((2, 2))] * 2,
+        ] + [pair] * 8 + [pltpu.SemaphoreType.DMA((2, 2))] * 2
+        + [pltpu.SemaphoreType.DMA((2, max(1, n // CORES)))] * 2
+        + [pltpu.SemaphoreType.DMA((2, n_lat))] * 2
+        + [pltpu.SemaphoreType.DMA((2,))] * 2,
         compiler_params=pltpu.CompilerParams(
             collective_id=0, has_side_effects=True, vmem_limit_bytes=50 * 2**20),
         name="convs",
     )(
         support, spread(field, 1), eye, forward, inverse, inverse_t,
-        spec_one, spread(theta_one, 0), spec_two, spread(theta_two, 0), spread(norm_gain, 0)[:, None],
+        spec_one, spread(theta_one, 0), spec_two, spread(theta_two, 0), spread(norm_gain, 0)[:, None], w_in, w_out,
     )
-    piece_in = lax.all_gather(w_in, "lon", axis=0, tiled=True)
-    piece_out = lax.all_gather(w_out, "lon", axis=0, tiled=True)
+    if gather:
+        piece_in, piece_out = piece_in.reshape(-1, chans), piece_out.reshape(-1, chans)
+    else:
+        piece_in = lax.all_gather(w_in, "lon", axis=0, tiled=True)
+        piece_out = lax.all_gather(w_out, "lon", axis=0, tiled=True)
     cells = out.reshape(n, lon_pad, rows, cp)[:, :lons, :, :part]
     cells = cells.transpose(2, 0, 3, 1).reshape(rows, chans, lons)
     hidden = jax.nn.gelu(

time: 88.6 us -> 74.7 us (0.84)
  between operations: 13.6 us -> 0.18 us
  local copies, waits for them, and re-layouts: 7.52 us -> 10.1 us
  waiting for transfers between devices: 1.42 us -> 0 us
  Pallas kernels: 60.6 us -> 59.6 us
    unnamed x28 -> x24, local copies, waits for them, and re-layouts: 4.31 us -> 6.16 us
    unnamed x2 -> x0, waiting for transfers between devices: 1.38 us -> none
    pallas_call x1, Pallas kernels: 60.6 us -> 59.6 us  [shards(): pl.pallas_call(functools.partial(conv_kernel, n, n_lat, chans, half, gath...]
  transfers between devices with their start and end apart: 2 -> 0, of which waited for: 0 -> 0; matrix products, arithmetic and copies ran while one was open for 6% -> 0% of each run, Pallas kernels for 69% -> 0%
where the time goes in v1:
time: 74.7 us; the launch traced here: 73.9 us
  Pallas kernels  59.6 us (80%)
  local copies, waits for them, and re-layouts  10.1 us (14%)
  matrix products  4.09 us (5%)
    pallas_call x1, Pallas kernels, shards(): pl.pallas_call(functools.partial(conv_kernel, n, n_lat, chans, half, gath...  59.6 us
    unnamed x24, local copies, waits for them, and re-layouts  6.16 us
    dot_general x1, matrix products, shards(): jnp.einsum('hfl,fc->hcl', hidden, piece_out, preferred_element_type=F32)  4.09 us
    reshape x1, local copies, waits for them, and re-layouts, shards(): cells = out.reshape(n, lon_pad, rows, cp)[:, :lons, :, :part]  1.53 us

profile of v1, /device:TPU:1, one launch (start us, length us, event | category | flops | bytes accessed | tf_op | source)
XLA Modules:
  0.0 73.9 jit_solution(15928023856223962428)
XLA Ops:
  0.0 0.0 copy-start.6
  0.0 0.8 %copy.21.support = s32[12,3]{1,0:T(8,128)S(1)} copy(s32[12,3]{0,1:T(4,128)} %param.14) | data formatting | bytes 288 | tf_op args[1]
  0.8 0.8 %copy.24.theta_one = f32[384,3]{1,0:T(8,128)S(1)} copy(f32[384,3]{0,1:T(4,128)} %param.16) | data formatting | bytes 9216 | tf_op args[3]
  1.7 0.0 copy-start
  1.7 0.0 copy-start.1
  1.7 0.0 copy-start.2
  1.7 0.0 copy-start.3
  1.7 0.0 copy-start.4
  1.7 0.0 copy-start.5
  1.7 0.9 %copy.26.theta_two = f32[384,3]{1,0:T(8,128)S(1)} copy(f32[384,3]{0,1:T(4,128)} %param.18) | data formatting | bytes 9216 | tf_op args[5]
  2.7 0.8 %broadcast_in_dim.4.gain = f32[384,1]{1,0:T(8,128)S(1)} reshape(f32[384]{0:T(512)} %param.19) | data formatting | bytes 3072 | tf_op jit(solution)/shard_map/broadcast_in_dim | solution.py:291
  3.5 1.0 %copy.23.spec_one = f32[2,3,12,3,180]{4,3,2,1,0:T(4,128)S(1)} copy(f32[2,3,12,3,180]{4,0,3,2,1:T(2,128)} %param.15) | data formatting | bytes 311040 | tf_op args[2]
  4.5 1.0 %copy.25.spec_two = f32[2,3,12,3,180]{4,3,2,1,0:T(4,128)S(1)} copy(f32[2,3,12,3,180]{4,0,3,2,1:T(2,128)} %param.17) | data formatting | bytes 311040 | tf_op args[4]
  5.5 0.0 copy-done.6
  5.5 1.5 %copy.22.field = bf16[12,384,45]{2,1,0:T(8,128)(2,1)} copy(bf16[12,384,45]{1,2,0:T(8,128)(2,1)S(1)} %copy-done.6) | data formatting | bytes 829440 | tf_op args[0]
  7.0 0.0 copy-done
  7.0 0.0 copy-done.1
  7.0 0.0 copy-done.2
  7.0 0.0 copy-done.3
  7.0 0.0 copy-done.4
  7.0 0.0 copy-done.5
  7.0 59.6 %convs.1 = (bf16[8,48,576]{2,1,0:T(8,128)(2,1)S(1)}, bf16[2,4,4,48,384]{4,3,2,1,0:T(8,128)(2,1)}, bf16[2,4,4,48,384]{4,3,2,1,0:T(8,128)(2,1)}) custom-call(s32[12,3]{1,0:T(8,128)S(1)} %copy.21.support, bf16[12,384,45]{2,1,0:T(8,128)(2,1)} %copy.22.field, bf16[48,45]{1,0:T(8,128)(2,1)S(1)} %copy-done.5, bf16[384,512]{1,0:T(8,128)(2,1)S(1)} %copy-done.2, ...), custom_call_target="tpu_custom_call" | custom-call | tf_op jit(solution)/shard_map/convs/pallas_call | solution.py:265
  66.6 1.5 %reshape.14 = bf16[8,48,12,48]{3,2,1,0:T(8,128)(2,1)S(1)} reshape(bf16[8,48,576]{2,1,0:T(8,128)(2,1)S(1)} %get-tuple-element.10) | data formatting | bytes 884736 | tf_op jit(solution)/shard_map/reshape | solution.py:298
  68.1 0.3 slice_bitcast_fusion
  68.4 0.0 copy-start.7
  68.4 0.0 copy-start.8
  68.4 0.3 copy.28
  68.7 1.0 %reshape.15 = bf16[12,384,45]{1,2,0:T(8,128)(2,1)S(1)} reshape(bf16[12,8,48,45]{2,1,3,0:T(8,128)(2,1)S(1)} %copy.28) | data formatting | bytes 829440 | tf_op jit(solution)/shard_map/reshape | solution.py:299
  69.8 0.0 copy-done.7
  69.8 0.1 copy-done.8
  69.8 4.1 %fusion.11 = bf16[12,384,45]{1,2,0:T(8,128)(2,1)} fusion(bf16[1536,384,1]{1,0,2:T(8,128)(2,1)} %bitcast.32, bf16[1536,384,1]{1,0,2:T(8,128)(2,1)S(1)} %bitcast.31, bf16[12,384,45]{1,2,0:T(8,128)(2,1)S(1)} %reshape.15, bf16[12,384,45]{1,2,0:T(8,128)(2,1)S(1)} %copy-done.7), kind=kOutput, calls=%fused_computation.13 | convolution fusion | flops 1282106880 | bytes 3603456 | tf_op jit(solution)/shard_map/hfl,fc->hcl/dot_general | solution.py:303
Async XLA Ops:
  0.0 5.5 %copy-start.6 = (bf16[12,384,45]{1,2,0:T(8,128)(2,1)S(1)}, bf16[12,384,45]{1,2,0:T(8,128)(2,1)}, u32[]{:S(2)}) copy-start(bf16[12,384,45]{1,2,0:T(8,128)(2,1)} %param.13) | copy-start | bytes 1244164
  1.7 5.3 %copy-start = (bf16[384,512]{1,0:T(8,128)(2,1)S(1)}, bf16[384,512]{1,0:T(8,128)(2,1)}, u32[]{:S(2)}) copy-start(bf16[384,512]{1,0:T(8,128)(2,1)} %constant.19.clone.inverse_t) | copy-start | bytes 1179652
  1.7 5.3 %copy-start.1 = (bf16[512,384]{1,0:T(8,128)(2,1)S(1)}, bf16[512,384]{1,0:T(8,128)(2,1)}, u32[]{:S(2)}) copy-start(bf16[512,384]{1,0:T(8,128)(2,1)} %constant.18.clone.inverse) | copy-start | bytes 1179652
  1.7 5.3 %copy-start.2 = (bf16[384,512]{1,0:T(8,128)(2,1)S(1)}, bf16[384,512]{1,0:T(8,128)(2,1)}, u32[]{:S(2)}) copy-start(bf16[384,512]{1,0:T(8,128)(2,1)} %constant.17.clone.forward) | copy-start | bytes 1179652
  1.7 5.3 %copy-start.3 = (bf16[192,384]{1,0:T(8,128)(2,1)S(1)}, bf16[192,384]{1,0:T(8,128)(2,1)}, u32[]{:S(2)}) copy-start(bf16[192,384]{1,0:T(8,128)(2,1)} %w_in.1) | copy-start | bytes 442372
  1.7 5.3 %copy-start.4 = (bf16[192,384]{1,0:T(8,128)(2,1)S(1)}, bf16[192,384]{1,0:T(8,128)(2,1)}, u32[]{:S(2)}) copy-start(bf16[192,384]{1,0:T(8,128)(2,1)} %w_out.1) | copy-start | bytes 442372
  1.7 5.3 %copy-start.5 = (bf16[48,45]{1,0:T(8,128)(2,1)S(1)}, bf16[48,45]{1,0:T(8,128)(2,1)}, u32[]{:S(2)}) copy-start(bf16[48,45]{1,0:T(8,128)(2,1)} %constant.16.clone.eye) | copy-start | bytes 12964
  68.4 1.4 %copy-start.7 = (bf16[12,384,45]{1,2,0:T(8,128)(2,1)S(1)}, bf16[12,384,45]{1,2,0:T(8,128)(2,1)}, u32[]{:S(2)}) copy-start(bf16[12,384,45]{1,2,0:T(8,128)(2,1)} %param.13) | copy-start | bytes 1244164
  68.4 1.4 %copy-start.8 = (bf16[2,4,4,48,384]{4,3,2,1,0:T(8,128)(2,1)S(1)}, bf16[2,4,4,48,384]{4,3,2,1,0:T(8,128)(2,1)}, u32[]{:S(2)}) copy-start(bf16[2,4,4,48,384]{4,3,2,1,0:T(8,128)(2,1)} %get-tuple-element.9) | copy-start | bytes 3538948

commit v2 on v1

--- a/solution.py
+++ b/solution.py
@@ -34,21 +34,22 @@
     inverse_t[:, :lons, 1, :half] = (-sin * weights).reshape(n, lons, half)
     forward = forward.reshape(n * lon_pad, 2 * mode_pad)
     inverse_t = inverse_t.reshape(n * lon_pad, 2 * mode_pad)
-    eye = np.eye(lon_pad, lons, dtype=np.float32)
-    return [jnp.asarray(t, BF16) for t in (eye, forward, inverse_t.T, inverse_t)]
+    return [jnp.asarray(t, BF16) for t in (forward, inverse_t.T, inverse_t)]
 
 
 def conv_kernel(
     n, n_lat, chans, half, gather,
-    support, field, eye, forward, inverse, inverse_t, spec_one, theta_one, spec_two, theta_two, gain, w_in, w_out,
+    support, field, forward, inverse, inverse_t, spec_one, theta_one, spec_two, theta_two, gain, w_in, w_out,
     out, all_in, all_out,
     send_t, circ_t, ext_one, ext_two, spectra, packed, first, part, sums, totals, second_t,
+    columns,
     a_send, a_recv, b_send, b_recv, c_send, c_recv, d_send, d_recv, h_send, h_recv,
     u_send, u_recv, v_send, v_recv, w_send, w_recv,
 ):
     rows = field.shape[0]
-    cp = field.shape[1] // n
-    lon_pad = eye.shape[0]
+    lons = field.shape[1]
+    cp = field.shape[2] // n
+    lon_pad = send_t.shape[1]
     mode_pad = forward.shape[1] // 2
     me = lax.axis_index("lon")
     lat = lax.axis_index("lat")
@@ -65,11 +66,6 @@
     for o in range(1, n_lat):
         pl.semaphore_signal(
             barrier, inc=1, device_id=(lax.rem(lat + o, n_lat), me), device_id_type=MESH)
-
-    def block_of(d):
-        x = field[:, pl.ds(pl.multiple_of(d * cp, 16), cp), :].reshape(rows * cp, field.shape[2])
-        turned = lax.dot_general(eye[...], x, (((1,), (1,)), ((), ())), preferred_element_type=F32)
-        return turned.astype(BF16)
 
     def exchange(srcs, dst, send, recv):
         copies = []
@@ -80,13 +76,20 @@
         return copies
 
     mine = pl.multiple_of(me * lon_pad, 16)
-    copies_a = exchange(lambda o: send_t.at[o], circ_t.at[pl.ds(mine, lon_pad)], a_send, a_recv)
-    for o in range(1, n):
-        send_t[o] = block_of(peer(o))
-        if o == 1:
-            pl.semaphore_wait(barrier, n + n_lat - 2)
-        copies_a[o - 1].start()
-    circ_t[pl.ds(mine, lon_pad)] = block_of(me)
+    copies_a = exchange(lambda o: send_t.at[peer(o)], circ_t.at[pl.ds(mine, lon_pad)], a_send, a_recv)
+    send_t[...] = jnp.zeros_like(send_t)
+    for i in range(rows):
+        x = field[i]
+        for d in range(n):
+            send_t[d, :lons, i * cp:(i + 1) * cp] = x[:, d * cp:(d + 1) * cp]
+    pl.semaphore_wait(barrier, n + n_lat - 2)
+    for copy in copies_a:
+        copy.start()
+    circ_t[pl.ds(mine, lon_pad)] = send_t[me]
+    basis = theta_one.shape[0]
+    stack = [theta_one[...], theta_two[...], gain[...]]
+    stack.append(jnp.zeros((round_up(2 * basis + 1, 8) - 2 * basis - 1, n * cp), F32))
+    columns[...] = jnp.concatenate(stack, axis=0).T
     packed[...] = jnp.zeros_like(packed)
     part[...] = jnp.zeros_like(part)
 
@@ -137,29 +140,35 @@
                 x, forward[...], preferred_element_type=F32).reshape(count, cp, 2 * mode_pad)
 
         dft(HALO, rows)
-        for copy in halos:
-            copy.wait_recv()
-        dft(0, HALO)
-        dft(HALO + rows, HALO)
-        th = theta[pl.ds(pl.multiple_of(me * cp, 8), cp), :]
-        cols = [th[:, b:b + 1] for b in range(th.shape[1])]
+        th = columns[pl.ds(pl.multiple_of(me * cp, 8), cp), :]
+        cols = [th[:, theta + b:theta + b + 1] for b in range(basis)]
 
         def row(i, carry):
             p_re = jnp.zeros((cp, half), F32)
             p_im = jnp.zeros((cp, half), F32)
-            for k in range(support.shape[1]):
-                r = jnp.clip(support[i, k] - lat * rows + HALO, 0, rows + 2 * HALO - 1)
+            for k in range(support.shape[0]):
+                r = jnp.clip(support[k, i] - lat * rows + HALO, 0, rows + 2 * HALO - 1)
                 g = spectra[r]
                 g_re, g_im = g[:, :half], g[:, mode_pad:mode_pad + half]
-                w_re = sum(cols[b] * spec[0, b, i][k:k + 1, :] for b in range(len(cols)))
-                w_im = sum(cols[b] * spec[1, b, i][k:k + 1, :] for b in range(len(cols)))
+                w_re = sum(cols[b] * spec[b, i, k][0:1, :] for b in range(len(cols)))
+                w_im = sum(cols[b] * spec[b, i, k][1:2, :] for b in range(len(cols)))
                 p_re += w_re * g_re - w_im * g_im
                 p_im += w_re * g_im + w_im * g_re
             packed[i, :, :half] = p_re.astype(BF16)
             packed[i, :, mode_pad:mode_pad + half] = p_im.astype(BF16)
             return carry
 
-        lax.fori_loop(0, rows, row, 0)
+        inner = (HALO, rows - HALO) if rows > 2 * HALO else (0, 0)
+        lax.fori_loop(inner[0], inner[1], row, 0)
+        for copy in halos:
+            copy.wait_recv()
+        dft(0, HALO)
+        dft(HALO + rows, HALO)
+        if inner[1]:
+            lax.fori_loop(0, HALO, row, 0)
+            lax.fori_loop(rows - HALO, rows, row, 0)
+        else:
+            lax.fori_loop(0, rows, row, 0)
         return packed[...].reshape(rows * cp, 2 * mode_pad)
 
     for copy in copies_a:
@@ -170,7 +179,7 @@
         copy.start()
     for copy in copies_u:
         copy.start()
-    spectrum = mix(ext_one, halo_one, spec_one, theta_one)
+    spectrum = mix(ext_one, halo_one, spec_one, 0)
     values = jnp.dot(spectrum, inverse[...], preferred_element_type=F32).astype(BF16)
     first[...] = values.reshape(first.shape)
 
@@ -195,7 +204,7 @@
         copy.start()
     for copy in copies_c:
         copy.wait_recv()
-    scale = gain[pl.ds(pl.multiple_of(me * cp, 8), cp), :]
+    scale = columns[pl.ds(pl.multiple_of(me * cp, 8), cp), :][:, 2 * basis:2 * basis + 1]
     halo_two = halo(ext_two, 1)
 
     def normalise(i):
@@ -213,7 +222,7 @@
         copy.start()
     for i in range(HALO, rows - HALO):
         normalise(i)
-    spectrum = mix(ext_two, halo_two, spec_two, theta_two)
+    spectrum = mix(ext_two, halo_two, spec_two, basis)
     second_t[...] = lax.dot_general(
         inverse_t[...], spectrum, (((1,), (1,)), ((), ())), preferred_element_type=F32
     ).astype(BF16).reshape(second_t.shape)
@@ -231,6 +240,27 @@
         copy.wait_send()
     for copy in halo_one + halo_two:
         copy.wait_send()
+
+
+def mlp_kernel(n, part, cp, blocks, field, w_in, w_out, result, cells):
+    rows, lons, chans = field.shape
+    lon_pad = blocks.shape[1]
+    for i in range(rows):
+        for s in range(n):
+            piece = blocks[s, :, i * cp:i * cp + part]
+            cells[i * lon_pad:(i + 1) * lon_pad, s * part:(s + 1) * part] = piece
+    chunk = 4 if rows % 4 == 0 else 1
+
+    for j in range(rows // chunk):
+        x = cells[j * chunk * lon_pad:(j + 1) * chunk * lon_pad, :]
+        hidden = lax.dot_general(
+            x, w_in[...], (((1,), (1,)), ((), ())), preferred_element_type=F32)
+        hidden = jax.nn.gelu(hidden).astype(BF16)
+        update = jnp.dot(hidden, w_out[...], preferred_element_type=F32)
+        update = update.reshape(chunk, lon_pad, chans)[:, :lons, :]
+        for q in range(chunk):
+            i = j * chunk + q
+            result[i] = (field[i].astype(F32) + update[q]).astype(BF16)
 
 
 def shards(n, n_lat, field, support, spec_one, theta_one, spec_two, theta_two, norm_gain, w_in, w_out):
@@ -241,7 +271,7 @@
     cp = round_up(part, 16)
     lon_pad = round_up(lons, 16)
     mode_pad = round_up(half, 128)
-    eye, forward, inverse, inverse_t = tables(circle, n, lons, lon_pad, mode_pad)
+    forward, inverse, inverse_t = tables(circle, n, lons, lon_pad, mode_pad)
 
     def spread(x, axis):
         if cp == part:
@@ -265,7 +295,7 @@
     out, piece_in, piece_out = pl.pallas_call(
         functools.partial(conv_kernel, n, n_lat, chans, half, gather),
         out_shape=(jax.ShapeDtypeStruct((n, lon_pad, rows * cp), BF16), weights, weights),
-        in_specs=[smem] + [vmem] * 12,
+        in_specs=[smem] + [vmem] * 11,
         out_specs=(vmem, vmem, vmem),
         scratch_shapes=[
             pltpu.VMEM((n, lon_pad, rows * cp), BF16),
@@ -279,6 +309,7 @@
             pltpu.VMEM((n, per, lanes), F32),
             pltpu.VMEM((n, per, lanes), F32),
             pltpu.VMEM((n, lon_pad, rows * cp), BF16),
+            pltpu.VMEM((n * cp, round_up(2 * theta_one.shape[1] + 1, 8)), F32),
         ] + [pair] * 8 + [pltpu.SemaphoreType.DMA((2, 2))] * 2
         + [pltpu.SemaphoreType.DMA((2, max(1, n // CORES)))] * 2
         + [pltpu.SemaphoreType.DMA((2, n_lat))] * 2
@@ -287,21 +318,26 @@
             collective_id=0, has_side_effects=True, vmem_limit_bytes=50 * 2**20),
         name="convs",
     )(
-        support, spread(field, 1), eye, forward, inverse, inverse_t,
-        spec_one, spread(theta_one, 0), spec_two, spread(theta_two, 0), spread(norm_gain, 0)[:, None], w_in, w_out,
+        support.T, spread(field.transpose(0, 2, 1), 2), forward, inverse, inverse_t,
+        spec_one.transpose(1, 2, 3, 0, 4), spread(theta_one.T, 1),
+        spec_two.transpose(1, 2, 3, 0, 4), spread(theta_two.T, 1),
+        spread(norm_gain[None, :], 1), w_in, w_out,
     )
     if gather:
         piece_in, piece_out = piece_in.reshape(-1, chans), piece_out.reshape(-1, chans)
     else:
         piece_in = lax.all_gather(w_in, "lon", axis=0, tiled=True)
         piece_out = lax.all_gather(w_out, "lon", axis=0, tiled=True)
-    cells = out.reshape(n, lon_pad, rows, cp)[:, :lons, :, :part]
-    cells = cells.transpose(2, 0, 3, 1).reshape(rows, chans, lons)
-    hidden = jax.nn.gelu(
-        jnp.einsum("hcl,fc->hfl", cells, piece_in, preferred_element_type=F32)
-    ).astype(BF16)
-    update = jnp.einsum("hfl,fc->hcl", hidden, piece_out, preferred_element_type=F32)
-    return (field.astype(F32) + update).astype(BF16)
+    result = pl.pallas_call(
+        functools.partial(mlp_kernel, n, part, cp),
+        out_shape=jax.ShapeDtypeStruct((rows, lons, chans), BF16),
+        in_specs=[vmem] * 4,
+        out_specs=vmem,
+        scratch_shapes=[pltpu.VMEM((rows * lon_pad, chans), BF16)],
+        compiler_params=pltpu.CompilerParams(vmem_limit_bytes=40 * 2**20),
+        name="mlp",
+    )(out, field.transpose(0, 2, 1), piece_in, piece_out)
+    return result.transpose(0, 2, 1)
 
 
 def solution(mesh):

time: 74.7 us -> 73.9 us (0.989)
  matrix products: 4.09 us -> 0 us
  Pallas kernels: 59.6 us -> 61.6 us
  local copies, waits for them, and re-layouts: 10.1 us -> 11.7 us
    unnamed x24, local copies, waits for them, and re-layouts: 6.16 us -> 11 us
    dot_general x1 -> x0, matrix products: 4.09 us -> none  [shards(): jnp.einsum('hfl,fc->hcl', hidden, piece_out, preferred_element_type=F32)]
    pallas_call x0 -> x1, Pallas kernels: none -> 3.54 us  [shards(): pl.pallas_call(functools.partial(mlp_kernel, n, part, cp), out_shape=jax....]
    reshape x2 -> x0, local copies, waits for them, and re-layouts: 2.56 us -> none  [the longest x1 1.53 us: shards(): cells = out.reshape(n, lon_pad, rows, cp)[:, :lons, :, :part]]
    pallas_call x1, Pallas kernels: 59.6 us -> 58.1 us  [shards(): pl.pallas_call(functools.partial(conv_kernel, n, n_lat, chans, half, gath...]
where the time goes in v2:
time: 73.9 us; the launch traced here: 73.3 us
  Pallas kernels  61.6 us (83%)
  local copies, waits for them, and re-layouts  11.7 us (16%)
    pallas_call x1, Pallas kernels, shards(): pl.pallas_call(functools.partial(conv_kernel, n, n_lat, chans, half, gath...  58.1 us
    unnamed x24, local copies, waits for them, and re-layouts  11 us
    pallas_call x1, Pallas kernels, shards(): pl.pallas_call(functools.partial(mlp_kernel, n, part, cp), out_shape=jax....  3.54 us

profile of v2, /device:TPU:1, one launch (start us, length us, event | category | flops | bytes accessed | tf_op | source)
XLA Modules:
  0.0 73.3 jit_solution(13309677747070210485)
XLA Ops:
  0.0 0.7 broadcast_in_dim.3.gain
  0.7 0.0 copy-start
  0.7 1.0 %copy-done = bf16[12,384,45]{1,2,0:T(8,128)(2,1)S(1)} copy-done((bf16[12,384,45]{1,2,0:T(8,128)(2,1)S(1)}, bf16[12,384,45]{1,2,0:T(8,128)(2,1)}, u32[]{:S(2)}) %copy-start) | copy-done | bytes 414744
  1.7 0.0 copy-start.2
  1.7 1.0 %copy-done.2 = bf16[384,512]{1,0:T(8,128)(2,1)S(1)} copy-done((bf16[384,512]{1,0:T(8,128)(2,1)S(1)}, bf16[384,512]{1,0:T(8,128)(2,1)}, u32[]{:S(2)}) %copy-start.2) | copy-done | bytes 393240
  2.7 0.0 copy-start.3
  2.7 1.0 %copy-done.3 = bf16[512,384]{1,0:T(8,128)(2,1)S(1)} copy-done((bf16[512,384]{1,0:T(8,128)(2,1)S(1)}, bf16[512,384]{1,0:T(8,128)(2,1)}, u32[]{:S(2)}) %copy-start.3) | copy-done | bytes 393240
  3.7 0.0 copy-start.4
  3.7 1.0 %copy-done.4 = bf16[384,512]{1,0:T(8,128)(2,1)S(1)} copy-done((bf16[384,512]{1,0:T(8,128)(2,1)S(1)}, bf16[384,512]{1,0:T(8,128)(2,1)}, u32[]{:S(2)}) %copy-start.4) | copy-done | bytes 393240
  4.7 0.0 copy-start.5
  4.7 0.9 %copy-done.5 = f32[2,3,12,3,180]{4,0,3,2,1:T(2,128)S(1)} copy-done((f32[2,3,12,3,180]{4,0,3,2,1:T(2,128)S(1)}, f32[2,3,12,3,180]{4,0,3,2,1:T(2,128)}, u32[]{:S(2)}) %copy-start.5) | copy-done | bytes 155544
  5.6 0.0 copy-start.6
  5.6 0.9 %copy-done.6 = f32[2,3,12,3,180]{4,0,3,2,1:T(2,128)S(1)} copy-done((f32[2,3,12,3,180]{4,0,3,2,1:T(2,128)S(1)}, f32[2,3,12,3,180]{4,0,3,2,1:T(2,128)}, u32[]{:S(2)}) %copy-start.6) | copy-done | bytes 155544
  6.6 0.0 copy-start.7
  6.6 0.9 %copy-done.7 = bf16[192,384]{1,0:T(8,128)(2,1)S(1)} copy-done((bf16[192,384]{1,0:T(8,128)(2,1)S(1)}, bf16[192,384]{1,0:T(8,128)(2,1)}, u32[]{:S(2)}) %copy-start.7) | copy-done | bytes 147480
  7.5 0.0 copy-start.8
  7.5 0.9 %copy-done.8 = bf16[192,384]{1,0:T(8,128)(2,1)S(1)} copy-done((bf16[192,384]{1,0:T(8,128)(2,1)S(1)}, bf16[192,384]{1,0:T(8,128)(2,1)}, u32[]{:S(2)}) %copy-start.8) | copy-done | bytes 147480
  8.4 0.0 copy-start.9
  8.4 0.7 copy-done.9
  9.1 0.0 copy-start.10
  9.1 0.7 copy-done.10
  9.8 0.0 copy-start.11
  9.8 0.7 copy-done.11
  10.4 58.1 %convs.1 = (bf16[8,48,576]{2,1,0:T(8,128)(2,1)S(1)}, bf16[2,4,4,48,384]{4,3,2,1,0:T(8,128)(2,1)S(1)}, bf16[2,4,4,48,384]{4,3,2,1,0:T(8,128)(2,1)}) custom-call(s32[3,12]{1,0:T(4,128)S(1)} %bitcast.17, bf16[12,45,384]{2,1,0:T(8,128)(2,1)S(1)} %bitcast.9, bf16[384,512]{1,0:T(8,128)(2,1)S(1)} %copy-done.4, bf16[512,384]{1,0:T(8,128)(2,1)S(1)} %copy-done.3, ...), custom_call_target="tpu_custom_call" | custom-call | tf_op jit(solution)/shard_map/convs/pallas_call | solution.py:295
  68.5 0.0 copy-start.1
  68.5 1.3 %copy-done.1 = bf16[2,4,4,48,384]{4,3,2,1,0:T(8,128)(2,1)S(1)} copy-done((bf16[2,4,4,48,384]{4,3,2,1,0:T(8,128)(2,1)S(1)}, bf16[2,4,4,48,384]{4,3,2,1,0:T(8,128)(2,1)}, u32[]{:S(2)}) %copy-start.1) | copy-done | bytes 1179672
  69.8 3.5 %mlp.1 = bf16[12,45,384]{2,1,0:T(8,128)(2,1)} custom-call(bf16[8,48,576]{2,1,0:T(8,128)(2,1)S(1)} %get-tuple-element.8.blocks, bf16[12,45,384]{2,1,0:T(8,128)(2,1)S(1)} %bitcast.10, bf16[1536,384]{1,0:T(8,128)(2,1)S(1)} %bitcast.11, bf16[1536,384]{1,0:T(8,128)(2,1)S(1)} %bitcast.12), custom_call_target="tpu_custom_call" | custom-call | tf_op jit(solution)/shard_map/mlp/pallas_call | solution.py:331
Async XLA Ops:
  0.7 1.0 %copy-start = (bf16[12,384,45]{1,2,0:T(8,128)(2,1)S(1)}, bf16[12,384,45]{1,2,0:T(8,128)(2,1)}, u32[]{:S(2)}) copy-start(bf16[12,384,45]{1,2,0:T(8,128)(2,1)} %param.12) | copy-start | bytes 1244164
  1.7 1.0 %copy-start.2 = (bf16[384,512]{1,0:T(8,128)(2,1)S(1)}, bf16[384,512]{1,0:T(8,128)(2,1)}, u32[]{:S(2)}) copy-start(bf16[384,512]{1,0:T(8,128)(2,1)} %constant.8.clone.inverse_t) | copy-start | bytes 1179652
  2.7 1.0 %copy-start.3 = (bf16[512,384]{1,0:T(8,128)(2,1)S(1)}, bf16[512,384]{1,0:T(8,128)(2,1)}, u32[]{:S(2)}) copy-start(bf16[512,384]{1,0:T(8,128)(2,1)} %constant.7.clone.inverse) | copy-start | bytes 1179652
  3.7 1.0 %copy-start.4 = (bf16[384,512]{1,0:T(8,128)(2,1)S(1)}, bf16[384,512]{1,0:T(8,128)(2,1)}, u32[]{:S(2)}) copy-start(bf16[384,512]{1,0:T(8,128)(2,1)} %constant.6.clone.forward) | copy-start | bytes 1179652
  4.7 0.9 %copy-start.5 = (f32[2,3,12,3,180]{4,0,3,2,1:T(2,128)S(1)}, f32[2,3,12,3,180]{4,0,3,2,1:T(2,128)}, u32[]{:S(2)}) copy-start(f32[2,3,12,3,180]{4,0,3,2,1:T(2,128)} %param.14) | copy-start | bytes 466564
  5.6 0.9 %copy-start.6 = (f32[2,3,12,3,180]{4,0,3,2,1:T(2,128)S(1)}, f32[2,3,12,3,180]{4,0,3,2,1:T(2,128)}, u32[]{:S(2)}) copy-start(f32[2,3,12,3,180]{4,0,3,2,1:T(2,128)} %param.16) | copy-start | bytes 466564
  6.6 0.9 %copy-start.7 = (bf16[192,384]{1,0:T(8,128)(2,1)S(1)}, bf16[192,384]{1,0:T(8,128)(2,1)}, u32[]{:S(2)}) copy-start(bf16[192,384]{1,0:T(8,128)(2,1)} %w_in.1) | copy-start | bytes 442372
  7.5 0.9 %copy-start.8 = (bf16[192,384]{1,0:T(8,128)(2,1)S(1)}, bf16[192,384]{1,0:T(8,128)(2,1)}, u32[]{:S(2)}) copy-start(bf16[192,384]{1,0:T(8,128)(2,1)} %w_out.1) | copy-start | bytes 442372
  8.4 0.7 copy-start.9
  9.1 0.7 copy-start.10
  9.8 0.7 copy-start.11
  68.5 1.3 %copy-start.1 = (bf16[2,4,4,48,384]{4,3,2,1,0:T(8,128)(2,1)S(1)}, bf16[2,4,4,48,384]{4,3,2,1,0:T(8,128)(2,1)}, u32[]{:S(2)}) copy-start(bf16[2,4,4,48,384]{4,3,2,1,0:T(8,128)(2,1)} %get-tuple-element.10) | copy-start | bytes 3538948

commit v3 on v2

--- a/solution.py
+++ b/solution.py
@@ -38,7 +38,7 @@
 
 
 def conv_kernel(
-    n, n_lat, chans, half, gather,
+    n, n_lat, chans, half, gather, loads,
     support, field, forward, inverse, inverse_t, spec_one, theta_one, spec_two, theta_two, gain, w_in, w_out,
     out, all_in, all_out,
     send_t, circ_t, ext_one, ext_two, spectra, packed, first, part, sums, totals, second_t,
@@ -78,6 +78,7 @@
     mine = pl.multiple_of(me * lon_pad, 16)
     copies_a = exchange(lambda o: send_t.at[peer(o)], circ_t.at[pl.ds(mine, lon_pad)], a_send, a_recv)
     send_t[...] = jnp.zeros_like(send_t)
+    loads[0].wait()
     for i in range(rows):
         x = field[i]
         for d in range(n):
@@ -86,6 +87,8 @@
     for copy in copies_a:
         copy.start()
     circ_t[pl.ds(mine, lon_pad)] = send_t[me]
+    for load in loads[1:]:
+        load.wait()
     basis = theta_one.shape[0]
     stack = [theta_one[...], theta_two[...], gain[...]]
     stack.append(jnp.zeros((round_up(2 * basis + 1, 8) - 2 * basis - 1, n * cp), F32))
@@ -242,13 +245,36 @@
         copy.wait_send()
 
 
-def mlp_kernel(n, part, cp, blocks, field, w_in, w_out, result, cells):
+def conv_entry(n, n_lat, chans, half, gather, count, support, gain, *refs):
+    held, rest = refs[:count], refs[count:-count - 1]
+    local, sems = refs[-count - 1:-1], refs[-1]
+    loads = [
+        pltpu.make_async_copy(src, dst, sems.at[k]) for k, (src, dst) in enumerate(zip(held, local))
+    ]
+    for load in loads:
+        load.start()
+    conv_kernel(
+        n, n_lat, chans, half, gather, loads, support, *local[:count - 2], gain, *local[count - 2:],
+        *rest)
+
+
+def mlp_kernel(
+    n, part, cp, blocks_at, field_at, w_in_at, w_out_at,
+    result, cells, blocks, field, w_in, w_out, sems,
+):
+    pairs = ((blocks_at, blocks), (w_in_at, w_in), (w_out_at, w_out), (field_at, field))
+    loads = [pltpu.make_async_copy(src, dst, sems.at[k]) for k, (src, dst) in enumerate(pairs)]
+    for load in loads:
+        load.start()
+    loads[0].wait()
     rows, lons, chans = field.shape
     lon_pad = blocks.shape[1]
     for i in range(rows):
         for s in range(n):
             piece = blocks[s, :, i * cp:i * cp + part]
             cells[i * lon_pad:(i + 1) * lon_pad, s * part:(s + 1) * part] = piece
+    for load in loads[1:]:
+        load.wait()
     chunk = 4 if rows % 4 == 0 else 1
 
     for j in range(rows // chunk):
@@ -292,10 +318,15 @@
     if not gather:
         piece = 16
     weights = jax.ShapeDtypeStruct((CORES, n_lat, n // CORES, piece, chans), BF16)
+    held = [
+        spread(field.transpose(0, 2, 1), 2), forward, inverse, inverse_t,
+        spec_one.transpose(1, 2, 3, 0, 4), spread(theta_one.T, 1),
+        spec_two.transpose(1, 2, 3, 0, 4), spread(theta_two.T, 1), w_in, w_out,
+    ]
     out, piece_in, piece_out = pl.pallas_call(
-        functools.partial(conv_kernel, n, n_lat, chans, half, gather),
+        functools.partial(conv_entry, n, n_lat, chans, half, gather, len(held)),
         out_shape=(jax.ShapeDtypeStruct((n, lon_pad, rows * cp), BF16), weights, weights),
-        in_specs=[smem] + [vmem] * 11,
+        in_specs=[smem, vmem] + [pl.BlockSpec(memory_space=pl.ANY)] * len(held),
         out_specs=(vmem, vmem, vmem),
         scratch_shapes=[
             pltpu.VMEM((n, lon_pad, rows * cp), BF16),
@@ -313,15 +344,13 @@
         ] + [pair] * 8 + [pltpu.SemaphoreType.DMA((2, 2))] * 2
         + [pltpu.SemaphoreType.DMA((2, max(1, n // CORES)))] * 2
         + [pltpu.SemaphoreType.DMA((2, n_lat))] * 2
-        + [pltpu.SemaphoreType.DMA((2,))] * 2,
+        + [pltpu.SemaphoreType.DMA((2,))] * 2
+        + [pltpu.VMEM(x.shape, x.dtype) for x in held] + [pltpu.SemaphoreType.DMA((len(held),))],
         compiler_params=pltpu.CompilerParams(
-            collective_id=0, has_side_effects=True, vmem_limit_bytes=50 * 2**20),
+            collective_id=0, has_side_effects=True, vmem_limit_bytes=60 * 2**20),
         name="convs",
     )(
-        support.T, spread(field.transpose(0, 2, 1), 2), forward, inverse, inverse_t,
-        spec_one.transpose(1, 2, 3, 0, 4), spread(theta_one.T, 1),
-        spec_two.transpose(1, 2, 3, 0, 4), spread(theta_two.T, 1),
-        spread(norm_gain[None, :], 1), w_in, w_out,
+        support.T, spread(norm_gain[None, :], 1), *held,
     )
     if gather:
         piece_in, piece_out = piece_in.reshape(-1, chans), piece_out.reshape(-1, chans)
@@ -331,10 +360,17 @@
     result = pl.pallas_call(
         functools.partial(mlp_kernel, n, part, cp),
         out_shape=jax.ShapeDtypeStruct((rows, lons, chans), BF16),
-        in_specs=[vmem] * 4,
+        in_specs=[pl.BlockSpec(memory_space=pl.ANY)] * 4,
         out_specs=vmem,
-        scratch_shapes=[pltpu.VMEM((rows * lon_pad, chans), BF16)],
-        compiler_params=pltpu.CompilerParams(vmem_limit_bytes=40 * 2**20),
+        scratch_shapes=[
+            pltpu.VMEM((rows * lon_pad, chans), BF16),
+            pltpu.VMEM(out.shape, BF16),
+            pltpu.VMEM((rows, lons, chans), BF16),
+            pltpu.VMEM(piece_in.shape, BF16),
+            pltpu.VMEM(piece_out.shape, BF16),
+            pltpu.SemaphoreType.DMA((4,)),
+        ],
+        compiler_params=pltpu.CompilerParams(vmem_limit_bytes=60 * 2**20),
         name="mlp",
     )(out, field.transpose(0, 2, 1), piece_in, piece_out)
     return result.transpose(0, 2, 1)

time: 73.9 us -> 66.2 us (0.90)
  local copies, waits for them, and re-layouts: 11.7 us -> 1.24 us
  Pallas kernels: 61.6 us -> 64.8 us
    unnamed x24 -> x0, local copies, waits for them, and re-layouts: 11 us -> none
    pallas_call x1, Pallas kernels: 3.54 us -> 5.15 us  [shards(): pl.pallas_call(functools.partial(mlp_kernel, n, part, cp), out_shape=jax....]
    pallas_call x1, Pallas kernels: 58.1 us -> 59.6 us  [shards(): pl.pallas_call(functools.partial(conv_entry, n, n_lat, chans, half, gathe...]
where the time goes in v3:
time: 66.2 us; the launch traced here: 66 us
  Pallas kernels  64.8 us (98%)
  local copies, waits for them, and re-layouts  1.24 us (2%)
    pallas_call x1, Pallas kernels, shards(): pl.pallas_call(functools.partial(conv_entry, n, n_lat, chans, half, gathe...  59.6 us
    pallas_call x1, Pallas kernels, shards(): pl.pallas_call(functools.partial(mlp_kernel, n, part, cp), out_shape=jax....  5.15 us

profile of v3, /device:TPU:1, one launch (start us, length us, event | category | flops | bytes accessed | tf_op | source)
XLA Modules:
  0.0 66.0 jit_solution(12092874862978565838)
XLA Ops:
  0.0 1.2 %broadcast_in_dim.3.gain = f32[1,384]{1,0:T(1,128)} reshape(f32[384]{0:T(512)} %param.18) | data formatting | bytes 3072 | tf_op jit(solution)/shard_map/broadcast_in_dim | solution.py:353
  1.2 59.6 %convs.1 = (bf16[8,48,576]{2,1,0:T(8,128)(2,1)}, bf16[2,4,4,48,384]{4,3,2,1,0:T(8,128)(2,1)}, bf16[2,4,4,48,384]{4,3,2,1,0:T(8,128)(2,1)}) custom-call(s32[3,12]{1,0:T(4,128)} %bitcast.17, f32[1,384]{1,0:T(1,128)} %broadcast_in_dim.3.gain, bf16[12,45,384]{2,1,0:T(8,128)(2,1)} %bitcast.9, bf16[384,512]{1,0:T(8,128)(2,1)} %constant.6.clone.refs_1_, ...), custom_call_target="tpu_custom_call" | custom-call | tf_op jit(solution)/shard_map/convs/pallas_call | solution.py:326
  60.9 5.1 %mlp.1 = bf16[12,45,384]{2,1,0:T(8,128)(2,1)} custom-call(bf16[8,48,576]{2,1,0:T(8,128)(2,1)} %get-tuple-element.8.blocks_at, bf16[12,45,384]{2,1,0:T(8,128)(2,1)} %bitcast.10, bf16[1536,384]{1,0:T(8,128)(2,1)} %bitcast.11, bf16[1536,384]{1,0:T(8,128)(2,1)} %bitcast.12), custom_call_target="tpu_custom_call" | custom-call | tf_op jit(solution)/shard_map/mlp/pallas_call | solution.py:360

commit v4 on v3

--- a/solution.py
+++ b/solution.py
@@ -90,7 +90,7 @@
     for load in loads[1:]:
         load.wait()
     basis = theta_one.shape[0]
-    stack = [theta_one[...], theta_two[...], gain[...]]
+    stack = [theta_one[...], theta_two[...], gain[...].reshape(1, n * cp)]
     stack.append(jnp.zeros((round_up(2 * basis + 1, 8) - 2 * basis - 1, n * cp), F32))
     columns[...] = jnp.concatenate(stack, axis=0).T
     packed[...] = jnp.zeros_like(packed)
@@ -226,15 +226,15 @@
     for i in range(HALO, rows - HALO):
         normalise(i)
     spectrum = mix(ext_two, halo_two, spec_two, basis)
+    for copy in copies_v:
+        copy.wait_recv()
+    for copy in copies_w:
+        copy.start()
     second_t[...] = lax.dot_general(
         inverse_t[...], spectrum, (((1,), (1,)), ((), ())), preferred_element_type=F32
     ).astype(BF16).reshape(second_t.shape)
     copies_d = exchange(lambda o: second_t.at[peer(o)], out.at[me], d_send, d_recv)
     for copy in copies_d:
-        copy.start()
-    for copy in copies_v:
-        copy.wait_recv()
-    for copy in copies_w:
         copy.start()
     out[me] = second_t[me]
     for copy in copies_d + copies_w:
@@ -350,7 +350,7 @@
             collective_id=0, has_side_effects=True, vmem_limit_bytes=60 * 2**20),
         name="convs",
     )(
-        support.T, spread(norm_gain[None, :], 1), *held,
+        support.T, spread(norm_gain, 0), *held,
     )
     if gather:
         piece_in, piece_out = piece_in.reshape(-1, chans), piece_out.reshape(-1, chans)

time: 66.2 us -> 65 us (0.982)
  local copies, waits for them, and re-layouts: 1.24 us -> 0 us
    broadcast_in_dim x1 -> x0, local copies, waits for them, and re-layouts: 1.24 us -> none  [shards(): norm_gain[None, :]]
where the time goes in v4:
time: 65 us; the launch traced here: 64.8 us
  Pallas kernels  64.8 us (100%)
    pallas_call x1, Pallas kernels, shards(): pl.pallas_call(functools.partial(conv_entry, n, n_lat, chans, half, gathe...  59.6 us
    pallas_call x1, Pallas kernels, shards(): pl.pallas_call(functools.partial(mlp_kernel, n, part, cp), out_shape=jax....  5.15 us

profile of v4, /device:TPU:1, one launch (start us, length us, event | category | flops | bytes accessed | tf_op | source)
XLA Modules:
  0.0 64.8 jit_solution(772029097513633468)
XLA Ops:
  0.0 59.6 %convs.1 = (bf16[8,48,576]{2,1,0:T(8,128)(2,1)}, bf16[2,4,4,48,384]{4,3,2,1,0:T(8,128)(2,1)}, bf16[2,4,4,48,384]{4,3,2,1,0:T(8,128)(2,1)}) custom-call(s32[3,12]{1,0:T(4,128)} %bitcast.17, f32[384]{0:T(512)} %gain.1, bf16[12,45,384]{2,1,0:T(8,128)(2,1)} %bitcast.9, bf16[384,512]{1,0:T(8,128)(2,1)} %constant.6.clone.refs_1_, ...), custom_call_target="tpu_custom_call" | custom-call | tf_op jit(solution)/shard_map/convs/pallas_call | solution.py:326
  59.6 5.1 %mlp.1 = bf16[12,45,384]{2,1,0:T(8,128)(2,1)} custom-call(bf16[8,48,576]{2,1,0:T(8,128)(2,1)} %get-tuple-element.8.blocks_at, bf16[12,45,384]{2,1,0:T(8,128)(2,1)} %bitcast.10, bf16[1536,384]{1,0:T(8,128)(2,1)} %bitcast.11, bf16[1536,384]{1,0:T(8,128)(2,1)} %bitcast.12), custom_call_target="tpu_custom_call" | custom-call | tf_op jit(solution)/shard_map/mlp/pallas_call | solution.py:360
